TPU v7x, 32 devices: a whole 2x2x4 slice. The times are simulated.
32 devices in a mesh: patch: 2 (over x), visit: 16 (over z, y, core).
Axes of the slice: x: 2, y: 2, z: 4, core: 2. Of those that a mesh axis runs over, the one named last changes fastest.
Arguments:
- template: bfloat16 [1024, 8192], P('visit', 'patch'), may hold values from -6 to 6
- science: bfloat16 [1024, 8192], P('visit', 'patch'), may hold values from -6 to 6
- row_shift: int32 [16, 2], P('visit', 'patch'), may hold values from -22 to 22, as said below
- col_shift: int32 [16, 2], P('visit', 'patch'), may hold values from -1024 to 1024, as said below
- valid_rows: int32 [16, 2], P('visit', 'patch'), may hold values from 32 to 64
- basis_rows: bfloat16 [9, 21], replicated, may hold values from -2.5 to 2.5
- basis_cols: bfloat16 [9, 21], replicated, may hold values from -2.5 to 2.5
- kernel_terms: float32 [16, 2, 9], P('visit', 'patch'), may hold values from -2.5 to 2.5
Outputs:
- patch_difference: float32 [1024, 8192], P('visit', 'patch')
Inputs may be any that keep to these rules, and one draw needn't show every extreme that they name: row_shift takes both its least and its largest value in every draw. col_shift takes both its least and its largest value in every draw.
All inputs are finite; a program needn't handle non-finite values.
Results may differ from a plain program's by a relative error of at most 0.0028.
Values may be sent and summed in bfloat16 or wider, within the bound.
A program may use at most 64 MiB of HBM per device.

v0:
```python
import jax
import jax.numpy as jnp
from jax import lax
from jax.sharding import PartitionSpec as P

DRIFT = 22
TILE = 128
COL_DRIFT = 1024


def passed_along(block, axis, distance):
    devices = range(lax.axis_size(axis))
    route = [(i - distance, i) for i in devices if i - distance in devices]
    return lax.ppermute(block, axis, route)


def with_halo(block, sides, width):
    for axis, dim in sides:
        count = lax.axis_size(axis)
        forward = [(i, i + 1) for i in range(count - 1)]
        backward = [(target, source) for source, target in forward]
        low = lax.ppermute(
            lax.slice_in_dim(block, block.shape[dim] - width, None, axis=dim), axis, forward
        )
        high = lax.ppermute(lax.slice_in_dim(block, 0, width, axis=dim), axis, backward)
        block = jnp.concatenate([low, block, high], axis=dim)
    return block


def band_tables(basis_rows, basis_cols, row_count, half_kernel, tile_width):
    taps = basis_rows.shape[1]
    terms = basis_rows.shape[0]
    distance = lax.broadcasted_iota(
        jnp.int32, (row_count, row_count + 2 * half_kernel), 1
    ) - lax.broadcasted_iota(jnp.int32, (row_count, row_count + 2 * half_kernel), 0)
    column_gap = lax.broadcasted_iota(
        jnp.int32, (tile_width + 2 * half_kernel, tile_width), 0
    ) - lax.broadcasted_iota(jnp.int32, (tile_width + 2 * half_kernel, tile_width), 1)
    vertical_band = jnp.zeros((terms, row_count, row_count + 2 * half_kernel), jnp.float32)
    horizontal_band = jnp.zeros((terms, tile_width + 2 * half_kernel, tile_width), jnp.float32)
    for tap_index in range(taps):
        vertical_band = (
            vertical_band
            + basis_rows[:, tap_index].astype(jnp.float32)[:, None, None]
            * (distance == tap_index).astype(jnp.float32)[None]
        )
        horizontal_band = (
            horizontal_band
            + basis_cols[:, tap_index].astype(jnp.float32)[:, None, None]
            * (column_gap == tap_index).astype(jnp.float32)[None]
        )
    return (vertical_band.astype(jnp.bfloat16), horizontal_band.astype(jnp.bfloat16))


def convolve(window, weights, vertical_band, horizontal_band, tile_width):
    row_count = vertical_band.shape[1]
    padded_cols = window.shape[1]
    twice_half = horizontal_band.shape[1] - tile_width
    col_count = padded_cols - twice_half
    tile_count = col_count // tile_width
    accumulated = jnp.zeros((row_count, tile_count, tile_width), jnp.float32)
    for basis_index in range(vertical_band.shape[0]):
        vertical = (
            jnp.dot(vertical_band[basis_index], window, preferred_element_type=jnp.float32)
            * weights[basis_index]
        )
        vertical = vertical.astype(jnp.bfloat16)
        extended = jnp.pad(vertical, ((0, 0), (0, (tile_count + 1) * tile_width - padded_cols)))
        blocks = extended.reshape(row_count, tile_count + 1, tile_width)
        accumulated = accumulated + jnp.einsum(
            "rtk,kj->rtj",
            blocks[:, :tile_count],
            horizontal_band[basis_index, :tile_width],
            preferred_element_type=jnp.float32,
        )
        accumulated = accumulated + jnp.einsum(
            "rtk,kj->rtj",
            blocks[:, 1:, :twice_half],
            horizontal_band[basis_index, tile_width:],
            preferred_element_type=jnp.float32,
        )
    return accumulated.reshape(row_count, col_count)


def fold_rows(frame, cover):
    core = frame.shape[0] - 2 * DRIFT
    lower_frame, lower_cover = passed_along((frame[:DRIFT], cover[:DRIFT]), "visit", -1)
    upper_frame, upper_cover = passed_along(
        (frame[core + DRIFT :], cover[core + DRIFT :]), "visit", 1
    )
    new_frame = (
        frame[DRIFT : DRIFT + core]
        + jnp.pad(lower_frame, ((core - DRIFT, 0), (0, 0)))
        + jnp.pad(upper_frame, ((0, core - DRIFT), (0, 0)))
    )
    new_cover = (
        cover[DRIFT : DRIFT + core]
        + jnp.pad(lower_cover, ((core - DRIFT, 0), (0, 0)))
        + jnp.pad(upper_cover, ((0, core - DRIFT), (0, 0)))
    )
    return (new_frame, new_cover)


def fold_cols(frame, cover):
    margin = COL_DRIFT
    core = frame.shape[1] - 2 * margin
    right_frame, right_cover = passed_along((frame[:, :margin], cover[:, :margin]), "patch", -1)
    left_frame, left_cover = passed_along(
        (frame[:, core + margin :], cover[:, core + margin :]), "patch", 1
    )
    new_frame = (
        frame[:, margin : margin + core]
        + jnp.pad(right_frame, ((0, 0), (core - margin, 0)))
        + jnp.pad(left_frame, ((0, 0), (0, core - margin)))
    )
    new_cover = (
        cover[:, margin : margin + core]
        + jnp.pad(right_cover, ((0, 0), (core - margin, 0)))
        + jnp.pad(left_cover, ((0, 0), (0, core - margin)))
    )
    return (new_frame, new_cover)


def body(template, science, row_shift, col_shift, valid_rows, basis_rows, basis_cols, kernel_terms):
    row_count = template.shape[0]
    col_count = template.shape[1]
    half_kernel = (basis_rows.shape[1] - 1) // 2
    reach_rows = DRIFT + half_kernel
    reach_cols = COL_DRIFT + half_kernel
    extended = with_halo(
        with_halo(template, (("visit", 0),), reach_rows), (("patch", 1),), reach_cols
    )
    shift_rows = row_shift[0, 0]
    shift_cols = col_shift[0, 0]
    window = lax.dynamic_slice(
        extended,
        (reach_rows + shift_rows - half_kernel, COL_DRIFT + shift_cols),
        (row_count + 2 * half_kernel, col_count + 2 * half_kernel),
    )
    vertical_band, horizontal_band = band_tables(
        basis_rows, basis_cols, row_count, half_kernel, TILE
    )
    convolved = convolve(window, kernel_terms[0, 0], vertical_band, horizontal_band, TILE)
    live_rows = jnp.arange(row_count, dtype=jnp.int32) < valid_rows[0, 0]
    difference = jnp.where(
        live_rows[:, None], science.astype(jnp.float32) - convolved, jnp.float32(0.0)
    )
    ones_block = jnp.broadcast_to(live_rows.astype(jnp.float32)[:, None], (row_count, col_count))
    frame_shape = (row_count + 2 * DRIFT, col_count + 2 * COL_DRIFT)
    position = (DRIFT + shift_rows, COL_DRIFT + shift_cols)
    frame = lax.dynamic_update_slice(jnp.zeros(frame_shape, jnp.float32), difference, position)
    cover = lax.dynamic_update_slice(jnp.zeros(frame_shape, jnp.float32), ones_block, position)
    frame, cover = fold_rows(frame, cover)
    frame, cover = fold_cols(frame, cover)
    return frame / jnp.maximum(cover, jnp.float32(1.0))


def solution(mesh):
    placed = (
        P("visit", "patch"),
        P("visit", "patch"),
        P("visit", "patch"),
        P("visit", "patch"),
        P("visit", "patch"),
        P(),
        P(),
        P("visit", "patch", None),
    )
    return jax.shard_map(
        body, mesh=mesh, in_specs=placed, out_specs=P("visit", "patch"), check_vma=False
    )
```

profile of v0, /device:TPU:22, one launch (start us, length us, event | category | flops | bytes accessed | tf_op | source)
XLA Modules:
  0.0 157.5 jit_solution(10708457151639500809)
XLA Ops:
  3.7 3.6 %collective-permute-start.1 = (bf16[32,4096]{1,0:T(8,128)(2,1)}, bf16[32,4096]{1,0:T(8,128)(2,1)}, u32[]{:S(2)}, u32[]{:S(2)}) collective-permute-start(bf16[32,4096]{1,0:T(8,128)(2,1)} %get-tuple-element.57), channel_id=1, source_target_pairs={{1,0},{2,1},{3,2},{4,3},{5,4},{6,5},{7,6},{8,7},{9,8},{10,9},{11,1... | collective-permute-start | bytes 786440 | tf_op jit(solution)/shard_map/ppermute | solution.py:25
  11.2 7.2 %dynamic_update_slice.7 = f32[108,6144]{1,0:T(8,128)S(1)} dynamic-update-slice(f32[108,6144]{1,0:T(8,128)S(1)} %broadcast.212.clone, f32[64,4096]{1,0:T(8,128)} %broadcast_in_dim.12, s32[]{:T(128)S(6)} %select_n.21, s32[]{:T(128)S(6)} %select_n.22) | dynamic-update-slice | bytes 2097156 | tf_op jit(solution)/shard_map/dynamic_update_slice | solution.py:152
  19.6 2.1 %collective-permute-start.8 = (f32[22,6144]{1,0:T(8,128)}, f32[22,6144]{1,0:T(8,128)}, u32[]{:S(2)}, u32[]{:S(2)}) collective-permute-start(f32[22,6144]{1,0:T(8,128)} %get-tuple-element.49), channel_id=1, source_target_pairs={{1,0},{2,1},{3,2},{4,3},{5,4},{6,5},{7,6},{8,7},{9,8},{10,9},{11,1... | collective-permute-start | bytes 1622024 | tf_op jit(solution)/shard_map/ppermute | solution.py:14
  21.7 2.4 %collective-permute-start.9 = (f32[22,6144]{1,0:T(8,128)}, f32[22,6144]{1,0:T(8,128)}, u32[]{:S(2)}, u32[]{:S(2)}) collective-permute-start(f32[22,6144]{1,0:T(8,128)} %get-tuple-element.50), channel_id=1, source_target_pairs={{0,1},{1,2},{2,3},{3,4},{4,5},{5,6},{6,7},{7,8},{8,9},{9,10},{10,1... | collective-permute-start | bytes 1622024 | tf_op jit(solution)/shard_map/ppermute | solution.py:14
  37.8 4.6 %collective-permute-start.3 = (bf16[128,1034]{1,0:T(8,128)(2,1)S(1)}, bf16[128,1034]{1,0:T(8,128)(2,1)S(1)}, u32[]{:S(2)}, u32[]{:S(2)}) collective-permute-start(bf16[128,1034]{1,0:T(8,128)(2,1)S(1)} %get-tuple-element.55), channel_id=1, source_target_pairs={{16,0},{17,1},{18,2},{19,3},{20,4},{21,5},{22,6},{23,7},{24,8},{25... | collective-permute-start | bytes 794120 | tf_op jit(solution)/shard_map/ppermute | solution.py:25
  43.3 4.0 %collective-permute-done.2 = bf16[128,1034]{1,0:T(8,128)(2,1)S(1)} collective-permute-done((bf16[128,1034]{1,0:T(8,128)(2,1)S(1)}, bf16[128,1034]{1,0:T(8,128)(2,1)S(1)}, u32[]{:S(2)}, u32[]{:S(2)}) %collective-permute-start.2) | collective-permute-done | bytes 264736 | tf_op jit(solution)/shard_map/ppermute | solution.py:22
  55.8 2.0 %fusion.49 = f32[64,32,128]{2,1,0:T(8,128)} fusion(bf16[64,33,128]{2,1,0:T(8,128)(2,1)S(1)} %reshape.619, bf16[9,148,128]{2,1,0:T(8,128)(2,1)} %add_convert_fusion), kind=kOutput, calls=%fused_computation.73 | convolution fusion | flops 67108864 | bytes 1605632 | tf_op jit(solution)/shard_map/rtk,kj->rtj/dot_general | solution.py:70
  57.8 2.3 %fusion.2 = bf16[64,4116]{1,0:T(8,128)(2,1)S(1)} fusion(f32[]{:T(128)} %bitcast.18, bf16[128,6164]{1,0:T(8,128)(2,1)} %copy-done, s32[]{:T(128)S(6)} %select_n.18, s32[]{:T(128)S(6)} %select_n.19, bf16[9,64,84]{2,1,0:T(8,128)(2,1)} %copy-done.16), kind=kOutput, calls=%fused_computation.11 | convolution fusion | flops 44782080 | bytes 1287176 | tf_op jit(solution)/shard_map/dot_general | solution.py:64
  60.5 2.0 %fusion.43 = f32[64,32,128]{2,1,0:T(8,128)} fusion(bf16[64,33,128]{2,1,0:T(8,128)(2,1)S(1)} %reshape.621, bf16[9,148,128]{2,1,0:T(8,128)(2,1)} %add_convert_fusion), kind=kOutput, calls=%fused_computation.67 | convolution fusion | flops 67108864 | bytes 1605632 | tf_op jit(solution)/shard_map/rtk,kj->rtj/dot_general | solution.py:70
  62.5 2.3 %fusion.3 = bf16[64,4116]{1,0:T(8,128)(2,1)S(1)} fusion(f32[]{:T(128)} %bitcast.24, bf16[128,6164]{1,0:T(8,128)(2,1)} %copy-done, s32[]{:T(128)S(6)} %select_n.18, s32[]{:T(128)S(6)} %select_n.19, bf16[9,64,84]{2,1,0:T(8,128)(2,1)} %copy-done.16), kind=kOutput, calls=%fused_computation.12 | convolution fusion | flops 44782080 | bytes 1287176 | tf_op jit(solution)/shard_map/dot_general | solution.py:64
  65.1 2.0 %fusion.40 = f32[64,32,128]{2,1,0:T(8,128)} fusion(bf16[64,33,128]{2,1,0:T(8,128)(2,1)S(1)} %reshape.622, bf16[9,148,128]{2,1,0:T(8,128)(2,1)} %add_convert_fusion), kind=kOutput, calls=%fused_computation.64 | convolution fusion | flops 67108864 | bytes 1605632 | tf_op jit(solution)/shard_map/rtk,kj->rtj/dot_general | solution.py:70
  67.2 2.4 %fusion.4 = bf16[64,4116]{1,0:T(8,128)(2,1)S(1)} fusion(f32[]{:T(128)} %bitcast.30, bf16[128,6164]{1,0:T(8,128)(2,1)} %copy-done, s32[]{:T(128)S(6)} %select_n.18, s32[]{:T(128)S(6)} %select_n.19, bf16[9,64,84]{2,1,0:T(8,128)(2,1)} %copy-done.16), kind=kOutput, calls=%fused_computation.13 | convolution fusion | flops 44782080 | bytes 1287176 | tf_op jit(solution)/shard_map/dot_general | solution.py:64
  71.7 2.1 %fusion.37 = f32[64,32,128]{2,1,0:T(8,128)} fusion(bf16[64,33,128]{2,1,0:T(8,128)(2,1)S(1)} %reshape.623, bf16[9,148,128]{2,1,0:T(8,128)(2,1)} %add_convert_fusion), kind=kOutput, calls=%fused_computation.61 | convolution fusion | flops 67108864 | bytes 1605632 | tf_op jit(solution)/shard_map/rtk,kj->rtj/dot_general | solution.py:70
  73.8 2.3 %fusion.5 = bf16[64,4116]{1,0:T(8,128)(2,1)S(1)} fusion(f32[]{:T(128)} %bitcast.36, bf16[128,6164]{1,0:T(8,128)(2,1)} %copy-done, s32[]{:T(128)S(6)} %select_n.18, s32[]{:T(128)S(6)} %select_n.19, bf16[9,64,84]{2,1,0:T(8,128)(2,1)} %copy-done.16), kind=kOutput, calls=%fused_computation.14 | convolution fusion | flops 44782080 | bytes 1287176 | tf_op jit(solution)/shard_map/dot_general | solution.py:64
  77.0 2.2 %reshape.624 = bf16[64,33,128]{2,1,0:T(8,128)(2,1)} reshape(bf16[64,4224]{1,0:T(8,128)(2,1)} %pad.61) | data formatting | bytes 1081344 | tf_op jit(solution)/shard_map/reshape | solution.py:69
  79.1 2.3 %fusion.34 = f32[64,32,128]{2,1,0:T(8,128)} fusion(bf16[64,33,128]{2,1,0:T(8,128)(2,1)} %reshape.624, bf16[9,148,128]{2,1,0:T(8,128)(2,1)} %add_convert_fusion), kind=kOutput, calls=%fused_computation.58 | convolution fusion | flops 67108864 | bytes 1605632 | tf_op jit(solution)/shard_map/rtk,kj->rtj/dot_general | solution.py:70
  81.4 2.4 %fusion.6 = bf16[64,4116]{1,0:T(8,128)(2,1)S(1)} fusion(f32[]{:T(128)} %bitcast.42, bf16[128,6164]{1,0:T(8,128)(2,1)} %copy-done, s32[]{:T(128)S(6)} %select_n.18, s32[]{:T(128)S(6)} %select_n.19, bf16[9,64,84]{2,1,0:T(8,128)(2,1)} %copy-done.16), kind=kOutput, calls=%fused_computation.15 | convolution fusion | flops 44782080 | bytes 1287176 | tf_op jit(solution)/shard_map/dot_general | solution.py:64
  84.6 2.2 %reshape.625 = bf16[64,33,128]{2,1,0:T(8,128)(2,1)} reshape(bf16[64,4224]{1,0:T(8,128)(2,1)} %pad.62) | data formatting | bytes 1081344 | tf_op jit(solution)/shard_map/reshape | solution.py:69
  86.8 2.3 %fusion.31 = f32[64,32,128]{2,1,0:T(8,128)} fusion(bf16[64,33,128]{2,1,0:T(8,128)(2,1)} %reshape.625, bf16[9,148,128]{2,1,0:T(8,128)(2,1)} %add_convert_fusion), kind=kOutput, calls=%fused_computation.55 | convolution fusion | flops 67108864 | bytes 1605632 | tf_op jit(solution)/shard_map/rtk,kj->rtj/dot_general | solution.py:70
  89.1 2.3 %fusion.7 = bf16[64,4116]{1,0:T(8,128)(2,1)S(1)} fusion(f32[]{:T(128)} %bitcast.48, bf16[128,6164]{1,0:T(8,128)(2,1)} %copy-done, s32[]{:T(128)S(6)} %select_n.18, s32[]{:T(128)S(6)} %select_n.19, bf16[9,64,84]{2,1,0:T(8,128)(2,1)} %copy-done.16), kind=kOutput, calls=%fused_computation.16 | convolution fusion | flops 44782080 | bytes 1287176 | tf_op jit(solution)/shard_map/dot_general | solution.py:64
  92.2 2.2 %reshape.626 = bf16[64,33,128]{2,1,0:T(8,128)(2,1)} reshape(bf16[64,4224]{1,0:T(8,128)(2,1)} %pad.63) | data formatting | bytes 1081344 | tf_op jit(solution)/shard_map/reshape | solution.py:69
  94.4 2.3 %fusion.28 = f32[64,32,128]{2,1,0:T(8,128)} fusion(bf16[64,33,128]{2,1,0:T(8,128)(2,1)} %reshape.626, bf16[9,148,128]{2,1,0:T(8,128)(2,1)} %add_convert_fusion), kind=kOutput, calls=%fused_computation.52 | convolution fusion | flops 67108864 | bytes 1605632 | tf_op jit(solution)/shard_map/rtk,kj->rtj/dot_general | solution.py:70
  96.7 2.4 %fusion.8 = bf16[64,4116]{1,0:T(8,128)(2,1)S(1)} fusion(f32[]{:T(128)} %bitcast.54, bf16[128,6164]{1,0:T(8,128)(2,1)} %copy-done, s32[]{:T(128)S(6)} %select_n.18, s32[]{:T(128)S(6)} %select_n.19, bf16[9,64,84]{2,1,0:T(8,128)(2,1)} %copy-done.16), kind=kOutput, calls=%fused_computation.17 | convolution fusion | flops 44782080 | bytes 1287176 | tf_op jit(solution)/shard_map/dot_general | solution.py:64
  99.9 2.2 %reshape.627 = bf16[64,33,128]{2,1,0:T(8,128)(2,1)} reshape(bf16[64,4224]{1,0:T(8,128)(2,1)} %pad.64) | data formatting | bytes 1081344 | tf_op jit(solution)/shard_map/reshape | solution.py:69
  117.2 7.2 %dynamic_update_slice.6 = f32[108,6144]{1,0:T(8,128)S(1)} dynamic-update-slice(f32[108,6144]{1,0:T(8,128)S(1)} %broadcast.212.clone.1, f32[64,4096]{1,0:T(8,128)} %fusion.19, s32[]{:T(128)S(6)} %select_n.21, s32[]{:T(128)S(6)} %select_n.22) | dynamic-update-slice | bytes 2097156 | tf_op jit(solution)/shard_map/dynamic_update_slice | solution.py:151
  126.5 2.4 %collective-permute-start.5 = (f32[22,6144]{1,0:T(8,128)S(1)}, f32[22,6144]{1,0:T(8,128)S(1)}, u32[]{:S(2)}, u32[]{:S(2)}) collective-permute-start(f32[22,6144]{1,0:T(8,128)S(1)} %get-tuple-element.48), channel_id=1, source_target_pairs={{0,1},{1,2},{2,3},{3,4},{4,5},{5,6},{6,7},{7,8},{8,9},{9,10},{10,1... | collective-permute-start | bytes 1622024 | tf_op jit(solution)/shard_map/ppermute | solution.py:14
  131.0 4.5 %collective-permute-start.10 = (f32[64,1024]{1,0:T(8,128)S(1)}, f32[64,1024]{1,0:T(8,128)S(1)}, u32[]{:S(2)}, u32[]{:S(2)}) collective-permute-start(f32[64,1024]{1,0:T(8,128)S(1)} %get-tuple-element.53), channel_id=1, source_target_pairs={{16,0},{17,1},{18,2},{19,3},{20,4},{21,5},{22,6},{23,7},{24,8},{25... | collective-permute-start | bytes 786440 | tf_op jit(solution)/shard_map/ppermute | solution.py:14
  136.8 3.4 %collective-permute-done.4 = f32[22,6144]{1,0:T(8,128)S(1)} collective-permute-done((f32[22,6144]{1,0:T(8,128)S(1)}, f32[22,6144]{1,0:T(8,128)S(1)}, u32[]{:S(2)}, u32[]{:S(2)}) %collective-permute-start.4) | collective-permute-done | bytes 540704 | tf_op jit(solution)/shard_map/ppermute | solution.py:14
  140.2 2.7 %collective-permute-done.5 = f32[22,6144]{1,0:T(8,128)S(1)} collective-permute-done((f32[22,6144]{1,0:T(8,128)S(1)}, f32[22,6144]{1,0:T(8,128)S(1)}, u32[]{:S(2)}, u32[]{:S(2)}) %collective-permute-start.5) | collective-permute-done | bytes 540704 | tf_op jit(solution)/shard_map/ppermute | solution.py:14
  143.2 4.9 %collective-permute-start.6 = (f32[64,1024]{1,0:T(8,128)S(1)}, f32[64,1024]{1,0:T(8,128)S(1)}, u32[]{:S(2)}, u32[]{:S(2)}) collective-permute-start(f32[64,1024]{1,0:T(8,128)S(1)} %get-tuple-element.51), channel_id=1, source_target_pairs={{16,0},{17,1},{18,2},{19,3},{20,4},{21,5},{22,6},{23,7},{24,8},{25... | collective-permute-start | bytes 786440 | tf_op jit(solution)/shard_map/ppermute | solution.py:14
  149.4 2.5 %collective-permute-done.6 = f32[64,1024]{1,0:T(8,128)S(1)} collective-permute-done((f32[64,1024]{1,0:T(8,128)S(1)}, f32[64,1024]{1,0:T(8,128)S(1)}, u32[]{:S(2)}, u32[]{:S(2)}) %collective-permute-start.6) | collective-permute-done | bytes 262176 | tf_op jit(solution)/shard_map/ppermute | solution.py:14
  151.9 4.4 %collective-permute-done.7 = f32[64,1024]{1,0:T(8,128)S(1)} collective-permute-done((f32[64,1024]{1,0:T(8,128)S(1)}, f32[64,1024]{1,0:T(8,128)S(1)}, u32[]{:S(2)}, u32[]{:S(2)}) %collective-permute-start.7) | collective-permute-done | bytes 262176 | tf_op jit(solution)/shard_map/ppermute | solution.py:14
  (162 shorter events, 58.5 us)
Async XLA Ops:
  1.8 32.5 %collective-permute-start = (bf16[32,4096]{1,0:T(8,128)(2,1)S(1)}, bf16[32,4096]{1,0:T(8,128)(2,1)}, u32[]{:S(2)}, u32[]{:S(2)}) collective-permute-start(bf16[32,4096]{1,0:T(8,128)(2,1)S(1)} %get-tuple-element.58), channel_id=1, source_target_pairs={{0,1},{1,2},{2,3},{3,4},{4,5},{5,6},{6,7},{7,8},{8,9},{9,10},{10,1... | collective-permute-start | bytes 786440 | tf_op jit(solution)/shard_map/ppermute | solution.py:22
  3.7 31.7 %collective-permute-start.1 = (bf16[32,4096]{1,0:T(8,128)(2,1)}, bf16[32,4096]{1,0:T(8,128)(2,1)}, u32[]{:S(2)}, u32[]{:S(2)}) collective-permute-start(bf16[32,4096]{1,0:T(8,128)(2,1)} %get-tuple-element.57), channel_id=1, source_target_pairs={{1,0},{2,1},{3,2},{4,3},{5,4},{6,5},{7,6},{8,7},{9,8},{10,9},{11,1... | collective-permute-start | bytes 786440 | tf_op jit(solution)/shard_map/ppermute | solution.py:25
  18.4 12.0 %copy-start.1 = (f32[108,6144]{1,0:T(8,128)}, f32[108,6144]{1,0:T(8,128)S(1)}, u32[]{:S(2)}) copy-start(f32[108,6144]{1,0:T(8,128)S(1)} %dynamic_update_slice.7) | copy-start | bytes 7962628
  19.6 11.0 %copy-start.14 = (bf16[9,21]{1,0:T(8,128)(2,1)S(1)}, bf16[9,21]{1,0:T(8,128)(2,1)}, u32[]{:S(2)}) copy-start(bf16[9,21]{1,0:T(8,128)(2,1)} %param.14) | copy-start | bytes 1138
  19.6 11.6 %copy-start.15 = (bf16[9,21]{1,0:T(8,128)(2,1)S(1)}, bf16[9,21]{1,0:T(8,128)(2,1)}, u32[]{:S(2)}) copy-start(bf16[9,21]{1,0:T(8,128)(2,1)} %param.13) | copy-start | bytes 1138
  19.6 11.9 %copy-start.36 = (f32[1,1,9]{2,1,0:T(1,128)S(1)}, f32[1,1,9]{2,1,0:T(1,128)}, u32[]{:S(2)}) copy-start(f32[1,1,9]{2,1,0:T(1,128)} %param.15) | copy-start | bytes 112
  19.6 109.3 %collective-permute-start.8 = (f32[22,6144]{1,0:T(8,128)}, f32[22,6144]{1,0:T(8,128)}, u32[]{:S(2)}, u32[]{:S(2)}) collective-permute-start(f32[22,6144]{1,0:T(8,128)} %get-tuple-element.49), channel_id=1, source_target_pairs={{1,0},{2,1},{3,2},{4,3},{5,4},{6,5},{7,6},{8,7},{9,8},{10,9},{11,1... | collective-permute-start | bytes 1622024 | tf_op jit(solution)/shard_map/ppermute | solution.py:14
  21.7 107.2 %collective-permute-start.9 = (f32[22,6144]{1,0:T(8,128)}, f32[22,6144]{1,0:T(8,128)}, u32[]{:S(2)}, u32[]{:S(2)}) collective-permute-start(f32[22,6144]{1,0:T(8,128)} %get-tuple-element.50), channel_id=1, source_target_pairs={{0,1},{1,2},{2,3},{3,4},{4,5},{5,6},{6,7},{7,8},{8,9},{9,10},{10,1... | collective-permute-start | bytes 1622024 | tf_op jit(solution)/shard_map/ppermute | solution.py:14
  34.1 8.5 %copy-start.21 = (f32[64,84]{1,0:T(8,128)S(1)}, f32[64,84]{1,0:T(8,128)}, u32[]{:S(2)}) copy-start(f32[64,84]{1,0:T(8,128)} %get-tuple-element.74) | copy-start | bytes 64516
  34.1 8.6 %copy-start.22 = (f32[64,84]{1,0:T(8,128)S(1)}, f32[64,84]{1,0:T(8,128)}, u32[]{:S(2)}) copy-start(f32[64,84]{1,0:T(8,128)} %get-tuple-element.75) | copy-start | bytes 64516
  34.1 8.6 %copy-start.23 = (f32[64,84]{1,0:T(8,128)S(1)}, f32[64,84]{1,0:T(8,128)}, u32[]{:S(2)}) copy-start(f32[64,84]{1,0:T(8,128)} %get-tuple-element.76) | copy-start | bytes 64516
  34.1 8.6 %copy-start.24 = (f32[64,84]{1,0:T(8,128)S(1)}, f32[64,84]{1,0:T(8,128)}, u32[]{:S(2)}) copy-start(f32[64,84]{1,0:T(8,128)} %get-tuple-element.77) | copy-start | bytes 64516
  34.1 8.6 %copy-start.25 = (f32[64,84]{1,0:T(8,128)S(1)}, f32[64,84]{1,0:T(8,128)}, u32[]{:S(2)}) copy-start(f32[64,84]{1,0:T(8,128)} %get-tuple-element.78) | copy-start | bytes 64516
  34.1 8.6 %copy-start.26 = (f32[64,84]{1,0:T(8,128)S(1)}, f32[64,84]{1,0:T(8,128)}, u32[]{:S(2)}) copy-start(f32[64,84]{1,0:T(8,128)} %get-tuple-element.79) | copy-start | bytes 64516
  34.2 8.6 %copy-start.27 = (f32[64,84]{1,0:T(8,128)S(1)}, f32[64,84]{1,0:T(8,128)}, u32[]{:S(2)}) copy-start(f32[64,84]{1,0:T(8,128)} %get-tuple-element.80) | copy-start | bytes 64516
  34.2 8.6 %copy-start.28 = (f32[64,84]{1,0:T(8,128)S(1)}, f32[64,84]{1,0:T(8,128)}, u32[]{:S(2)}) copy-start(f32[64,84]{1,0:T(8,128)} %get-tuple-element.81) | copy-start | bytes 64516
  34.2 8.6 %copy-start.29 = (f32[64,84]{1,0:T(8,128)S(1)}, f32[64,84]{1,0:T(8,128)}, u32[]{:S(2)}) copy-start(f32[64,84]{1,0:T(8,128)} %get-tuple-element.82) | copy-start | bytes 64516
  34.2 8.6 %copy-start.30 = (f32[64,84]{1,0:T(8,128)S(1)}, f32[64,84]{1,0:T(8,128)}, u32[]{:S(2)}) copy-start(f32[64,84]{1,0:T(8,128)} %get-tuple-element.83) | copy-start | bytes 64516
  34.2 8.6 %copy-start.31 = (f32[64,84]{1,0:T(8,128)S(1)}, f32[64,84]{1,0:T(8,128)}, u32[]{:S(2)}) copy-start(f32[64,84]{1,0:T(8,128)} %get-tuple-element.84) | copy-start | bytes 64516
  34.2 8.6 %copy-start.32 = (f32[64,84]{1,0:T(8,128)S(1)}, f32[64,84]{1,0:T(8,128)}, u32[]{:S(2)}) copy-start(f32[64,84]{1,0:T(8,128)} %get-tuple-element.85) | copy-start | bytes 64516
  34.2 8.6 %copy-start.33 = (f32[64,84]{1,0:T(8,128)S(1)}, f32[64,84]{1,0:T(8,128)}, u32[]{:S(2)}) copy-start(f32[64,84]{1,0:T(8,128)} %get-tuple-element.86) | copy-start | bytes 64516
  34.2 8.6 %copy-start.34 = (f32[64,84]{1,0:T(8,128)S(1)}, f32[64,84]{1,0:T(8,128)}, u32[]{:S(2)}) copy-start(f32[64,84]{1,0:T(8,128)} %get-tuple-element.87) | copy-start | bytes 64516
  34.2 8.6 %copy-start.35 = (f32[64,84]{1,0:T(8,128)S(1)}, f32[64,84]{1,0:T(8,128)}, u32[]{:S(2)}) copy-start(f32[64,84]{1,0:T(8,128)} %fusion.143) | copy-start | bytes 64516
  36.5 10.9 %collective-permute-start.2 = (bf16[128,1034]{1,0:T(8,128)(2,1)S(1)}, bf16[128,1034]{1,0:T(8,128)(2,1)S(1)}, u32[]{:S(2)}, u32[]{:S(2)}) collective-permute-start(bf16[128,1034]{1,0:T(8,128)(2,1)S(1)} %get-tuple-element.56), channel_id=1, source_target_pairs={{0,16},{1,17},{2,18},{3,19},{4,20},{5,21},{6,22},{7,23},{8,24},{9,... | collective-permute-start | bytes 794120 | tf_op jit(solution)/shard_map/ppermute | solution.py:22
  37.8 11.4 %collective-permute-start.3 = (bf16[128,1034]{1,0:T(8,128)(2,1)S(1)}, bf16[128,1034]{1,0:T(8,128)(2,1)S(1)}, u32[]{:S(2)}, u32[]{:S(2)}) collective-permute-start(bf16[128,1034]{1,0:T(8,128)(2,1)S(1)} %get-tuple-element.55), channel_id=1, source_target_pairs={{16,0},{17,1},{18,2},{19,3},{20,4},{21,5},{22,6},{23,7},{24,8},{25... | collective-permute-start | bytes 794120 | tf_op jit(solution)/shard_map/ppermute | solution.py:25
  43.3 8.9 %copy-start.16 = (bf16[9,64,84]{2,1,0:T(8,128)(2,1)}, bf16[9,64,84]{2,1,0:T(8,128)(2,1)S(1)}, u32[]{:S(2)}) copy-start(bf16[9,64,84]{2,1,0:T(8,128)(2,1)S(1)} %add_convert_fusion.1) | copy-start | bytes 290308
  124.6 15.6 %collective-permute-start.4 = (f32[22,6144]{1,0:T(8,128)S(1)}, f32[22,6144]{1,0:T(8,128)S(1)}, u32[]{:S(2)}, u32[]{:S(2)}) collective-permute-start(f32[22,6144]{1,0:T(8,128)S(1)} %get-tuple-element.47), channel_id=1, source_target_pairs={{1,0},{2,1},{3,2},{4,3},{5,4},{6,5},{7,6},{8,7},{9,8},{10,9},{11,1... | collective-permute-start | bytes 1622024 | tf_op jit(solution)/shard_map/ppermute | solution.py:14
  126.5 16.4 %collective-permute-start.5 = (f32[22,6144]{1,0:T(8,128)S(1)}, f32[22,6144]{1,0:T(8,128)S(1)}, u32[]{:S(2)}, u32[]{:S(2)}) collective-permute-start(f32[22,6144]{1,0:T(8,128)S(1)} %get-tuple-element.48), channel_id=1, source_target_pairs={{0,1},{1,2},{2,3},{3,4},{4,5},{5,6},{6,7},{7,8},{8,9},{9,10},{10,1... | collective-permute-start | bytes 1622024 | tf_op jit(solution)/shard_map/ppermute | solution.py:14
  131.0 18.4 %collective-permute-start.10 = (f32[64,1024]{1,0:T(8,128)S(1)}, f32[64,1024]{1,0:T(8,128)S(1)}, u32[]{:S(2)}, u32[]{:S(2)}) collective-permute-start(f32[64,1024]{1,0:T(8,128)S(1)} %get-tuple-element.53), channel_id=1, source_target_pairs={{16,0},{17,1},{18,2},{19,3},{20,4},{21,5},{22,6},{23,7},{24,8},{25... | collective-permute-start | bytes 786440 | tf_op jit(solution)/shard_map/ppermute | solution.py:14
  135.5 13.9 %collective-permute-start.11 = (f32[64,1024]{1,0:T(8,128)S(1)}, f32[64,1024]{1,0:T(8,128)S(1)}, u32[]{:S(2)}, u32[]{:S(2)}) collective-permute-start(f32[64,1024]{1,0:T(8,128)S(1)} %get-tuple-element.54), channel_id=1, source_target_pairs={{0,16},{1,17},{2,18},{3,19},{4,20},{5,21},{6,22},{7,23},{8,24},{9,... | collective-permute-start | bytes 786440 | tf_op jit(solution)/shard_map/ppermute | solution.py:14
  143.2 8.8 %collective-permute-start.6 = (f32[64,1024]{1,0:T(8,128)S(1)}, f32[64,1024]{1,0:T(8,128)S(1)}, u32[]{:S(2)}, u32[]{:S(2)}) collective-permute-start(f32[64,1024]{1,0:T(8,128)S(1)} %get-tuple-element.51), channel_id=1, source_target_pairs={{16,0},{17,1},{18,2},{19,3},{20,4},{21,5},{22,6},{23,7},{24,8},{25... | collective-permute-start | bytes 786440 | tf_op jit(solution)/shard_map/ppermute | solution.py:14
  148.1 8.3 %collective-permute-start.7 = (f32[64,1024]{1,0:T(8,128)S(1)}, f32[64,1024]{1,0:T(8,128)S(1)}, u32[]{:S(2)}, u32[]{:S(2)}) collective-permute-start(f32[64,1024]{1,0:T(8,128)S(1)} %get-tuple-element.52), channel_id=1, source_target_pairs={{0,16},{1,17},{2,18},{3,19},{4,20},{5,21},{6,22},{7,23},{8,24},{9,... | collective-permute-start | bytes 786440 | tf_op jit(solution)/shard_map/ppermute | solution.py:14
  (18 other events, 48.1 us)
where the time goes:
time: 160 us; the launch traced here: 158 us
  matrix products  47.4 us (30%)
  local copies, waits for them, and re-layouts  40.4 us (25%)
  starting transfers between devices  32.1 us (20%)
  waiting for transfers between devices  19 us (12%)
  other arithmetic  15.8 us (10%)
  between operations  2.87 us (2%)
    ppermute x8, starting transfers between devices, passed_along(): return lax.ppermute(block, axis, route)  20.7 us
    dot_general x9, matrix products, convolve(): jnp.dot(vertical_band[basis_index], window, preferred_element_type=jnp.fl...  18.7 us
    dot_general x9, matrix products, convolve(): jnp.einsum('rtk,kj->rtj', blocks[:, :tile_count], horizontal_band[basis_i...  18.5 us
    ppermute x8, waiting for transfers between devices, passed_along(): return lax.ppermute(block, axis, route)  13.1 us
    reshape x9, local copies, waits for them, and re-layouts, convolve(): blocks = extended.reshape(row_count, tile_count + 1, tile_width)  11 us
    dot_general x9, matrix products, convolve(): jnp.einsum('rtk,kj->rtj', blocks[:, 1:, :twice_half], horizontal_band[bas...  10.2 us
    ppermute x2, starting transfers between devices, with_halo(): lax.ppermute(lax.slice_in_dim(block, 0, width, axis=dim), axis, backward)  8.22 us
    dynamic_update_slice x1, local copies, waits for them, and re-layouts, body(): lax.dynamic_update_slice(jnp.zeros(frame_shape, jnp.float32), ones_block,...  7.21 us
  transfers between devices with their start and end apart: 12, of which 6 were waited for; matrix products, arithmetic and copies ran while one was open for 63% of the time, Pallas kernels for 0%

commit v1 on v0

v1 whole, which is shorter than its diff:
```python
import functools

import jax
import jax.numpy as jnp
from jax import lax
from jax.experimental import pallas as pl
from jax.experimental.pallas import tpu as pltpu
from jax.sharding import PartitionSpec as P

DRIFT = 22
COL_DRIFT = 1024
MESH = pl.DeviceIdType.MESH
LANES = 128
TEDGE = 16
SEDGE = 32
SIDE = 24
TILE = 256
F32, BF16, I32 = jnp.float32, jnp.bfloat16, jnp.int32


def slot_of(dv, dp):
    return (dv + 1) * 3 + dp + 1


AROUND = [(dv, dp) for dv in (-1, 0, 1) for dp in (-1, 0, 1) if (dv, dp) != (0, 0)]


def plan(p, np_, chunks):
    has_left, has_right = (p > 0).astype(I32), (p < np_ - 1).astype(I32)
    passes = chunks + has_left + has_right

    def which(q):
        extra = q - chunks
        left = jnp.logical_and(extra == 0, has_left == 1)
        main = extra < 0
        c = jnp.where(main, q, jnp.where(left, 0, chunks - 1))
        dp = jnp.where(main, 0, jnp.where(left, -1, 1))
        return c, dp

    return passes, which


def kernel(
    np_, nv, template, science, row_shift, col_shift, valid_rows, basis_rows, basis_cols, terms,
    conv, moved, par_i, text, sky, par_f, sm_i, sm_f, taps, band_v, band_h, weighted,
    send_sem, recv_sem, local_sem,
):
    rows, width = template.shape
    terms_n, ksize = basis_rows.shape
    half = (ksize - 1) // 2
    group = rows + 2 * SIDE
    chunk = COL_DRIFT
    chunks = width // chunk
    tiles = chunk // TILE
    p, v = lax.axis_index("patch"), lax.axis_index("visit")

    def there(dv, dp):
        ok = None
        for cond, d in (
            (v > 0, dv == -1), (v < nv - 1, dv == 1), (p > 0, dp == -1), (p < np_ - 1, dp == 1)
        ):
            if d:
                ok = cond if ok is None else jnp.logical_and(ok, cond)
        return ok

    lane = lax.broadcasted_iota(I32, (1, LANES), 1)
    par_i[...] = jnp.zeros_like(par_i)
    par_f[...] = jnp.zeros_like(par_f)
    ints = jnp.where(
        lane == 0, row_shift[0, 0], jnp.where(lane == 1, col_shift[0, 0], jnp.where(lane == 2, valid_rows[0, 0], 0))
    )
    par_i[4] = ints
    floats = jnp.zeros((1, LANES), F32)
    for b in range(terms_n):
        floats = jnp.where(lane == b, terms[0, 0, b], floats)
    par_f[4] = floats

    own_t = pltpu.make_async_copy(
        template, text.at[pl.ds(TEDGE, rows), pl.ds(LANES, width)], local_sem.at[0]
    )
    own_s = pltpu.make_async_copy(
        science, sky.at[pl.ds(SEDGE, rows), pl.ds(COL_DRIFT, width)], local_sem.at[1]
    )
    own_t.start()
    own_s.start()

    barrier = pltpu.get_barrier_semaphore()
    for dv, dp in AROUND:
        @pl.when(there(dv, dp))
        def _():
            pl.semaphore_signal(
                barrier, inc=1, device_id={"patch": p + dp, "visit": v + dv}, device_id_type=MESH
            )
    one = lambda c: c.astype(I32)
    n_v = one(v > 0) + one(v < nv - 1)
    n_p = one(p > 0) + one(p < np_ - 1)
    pl.semaphore_wait(barrier, n_v + n_p + n_v * n_p)

    def span(d, edge, size):
        return {-1: (size - edge, 0, edge), 0: (0, edge, size), 1: (0, edge + size, edge)}[d]

    def regions(kind, dv, dp):
        if kind == 0:
            return par_i.at[4], par_i.at[slot_of(dv, dp)]
        if kind == 1:
            return par_f.at[4], par_f.at[slot_of(dv, dp)]
        src, dst, re, ce = (
            (template, text, TEDGE, LANES) if kind == 2 else (science, sky, SEDGE, COL_DRIFT)
        )
        r_src, r_dst, r_n = span(dv, re, rows)
        c_src, c_dst, c_n = span(dp, ce, width)
        return (
            src.at[pl.ds(r_src, r_n), pl.ds(c_src, c_n)],
            dst.at[pl.ds(r_dst, r_n), pl.ds(c_dst, c_n)],
        )

    def sending(kind, ev, ep):
        src, dst = regions(kind, -ev, -ep)
        return pltpu.make_async_remote_copy(
            src_ref=src, dst_ref=dst,
            send_sem=send_sem.at[kind, slot_of(ev, ep)],
            recv_sem=recv_sem.at[kind, slot_of(-ev, -ep)],
            device_id={"patch": p + ep, "visit": v + ev}, device_id_type=MESH,
        )

    def receiving(kind, dv, dp):
        _, dst = regions(kind, dv, dp)
        return pltpu.make_async_remote_copy(
            src_ref=dst, dst_ref=dst,
            send_sem=send_sem.at[kind, slot_of(dv, dp)],
            recv_sem=recv_sem.at[kind, slot_of(dv, dp)],
            device_id={"patch": p + dp, "visit": v + dv}, device_id_type=MESH,
        )

    for kinds in ((0, 1, 2), (3,)):
        for kind in kinds:
            for ev, ep in AROUND:
                @pl.when(there(ev, ep))
                def _():
                    sending(kind, ev, ep).start()

    for kind in (2, 3):
        for dv, dp in AROUND:
            @pl.when(jnp.logical_not(there(dv, dp)))
            def _():
                _, dst = regions(kind, dv, dp)
                dst[...] = jnp.zeros(dst.shape, BF16)

    taps[...] = jnp.zeros_like(taps)
    taps[0, 0:terms_n, 0:ksize] = basis_rows[...].astype(F32)
    taps[1, 0:terms_n, 0:ksize] = basis_cols[...].astype(F32)
    kk = lax.broadcasted_iota(I32, (LANES, LANES), 0)
    nn = lax.broadcasted_iota(I32, (LANES, LANES), 1)
    gap = kk - nn + half
    inside = [jnp.logical_and(gap + o >= 0, gap + o < ksize) for o in (-LANES, 0, LANES)]
    zero = jnp.zeros((LANES, LANES), BF16)
    turned_cols = pltpu.roll(taps[1], LANES - half, 1)
    for b in range(terms_n):
        row = jnp.broadcast_to(taps[0, b : b + 1, :], (rows, LANES))
        band_v[b * rows : (b + 1) * rows, :] = pltpu.roll(
            row, TEDGE - half, 1, stride=1, stride_axis=0
        ).astype(BF16)
        col = jnp.broadcast_to(turned_cols[b : b + 1, :], (LANES, LANES))
        mat = pltpu.roll(col, 0, 1, stride=1, stride_axis=0).T
        low, mid, top = [jnp.where(m, mat, 0.0).astype(BF16) for m in inside]
        at = b * TILE
        band_h[0, at : at + LANES, :] = jnp.concatenate([low, zero], axis=1)
        band_h[0, at + LANES : at + TILE, :] = jnp.concatenate([mid, low], axis=1)
        band_h[1, at : at + LANES, :] = jnp.concatenate([top, mid], axis=1)
        band_h[1, at + LANES : at + TILE, :] = jnp.concatenate([zero, top], axis=1)

    for kind in (0, 1, 2):
        for dv, dp in AROUND:
            @pl.when(there(dv, dp))
            def _():
                receiving(kind, dv, dp).wait_recv()
    to_i = pltpu.make_async_copy(par_i, sm_i, local_sem.at[2])
    to_f = pltpu.make_async_copy(par_f, sm_f, local_sem.at[3])
    to_i.start()
    to_f.start()
    own_t.wait()
    to_i.wait()
    to_f.wait()

    passes, which = plan(p, np_, chunks)

    @pl.loop(0, passes)
    def _(q):
        c, dp = which(q)
        for n in range(tiles + 1):
            start = pl.multiple_of(c * chunk + n * TILE, TILE)
            vert = jnp.dot(
                band_v[:, : rows + 2 * TEDGE], text[:, pl.ds(start, TILE)],
                preferred_element_type=F32,
            )
            for b in range(terms_n):
                mid_w = sm_f[4 + dp, 0, b]
                up_w = sm_f[1 + dp, 0, b]
                down_w = sm_f[7 + dp, 0, b]
                blk = vert[b * rows : (b + 1) * rows]
                at = n * group
                weighted[at : at + rows, b * TILE : (b + 1) * TILE] = (blk * mid_w).astype(BF16)
                weighted[at + rows : at + group, b * TILE : (b + 1) * TILE] = jnp.concatenate(
                    [blk[:SIDE] * up_w, blk[rows - SIDE :] * down_w], axis=0
                ).astype(BF16)
        conv[q] = jnp.dot(
            weighted[0 : tiles * group, :], band_h[0], preferred_element_type=F32
        ) + jnp.dot(
            weighted[group : (tiles + 1) * group, :], band_h[1], preferred_element_type=F32
        )

    own_s.wait()
    for dv, dp in AROUND:
        @pl.when(there(dv, dp))
        def _():
            receiving(3, dv, dp).wait_recv()

    def pick(dp):
        parts = []
        for dv, first, n in ((0, 0, rows), (-1, 0, SIDE), (1, rows - SIDE, SIDE)):
            y = lax.broadcasted_iota(I32, (n, rows + 2 * SEDGE), 0) + first
            j = lax.broadcasted_iota(I32, (n, rows + 2 * SEDGE), 1)
            rs = sm_i[slot_of(dv, dp), 0, 0]
            parts.append((j == y + SEDGE - rs).astype(F32))
        return jnp.concatenate(parts, axis=0).astype(BF16)

    for dp, first, n in ((-1, 0, COL_DRIFT), (0, COL_DRIFT, width), (1, COL_DRIFT + width, COL_DRIFT)):
        chosen = pick(dp)
        for k in range(n // TILE):
            at = first + k * TILE
            moved[:, at : at + TILE] = jnp.dot(
                chosen, sky[:, at : at + TILE], preferred_element_type=F32
            )

    for kind in range(4):
        for ev, ep in AROUND:
            @pl.when(there(ev, ep))
            def _():
                sending(kind, ev, ep).wait_send()


def gather_kernel(np_, conv, moved, par_i, out, count, sm_i, sem):
    rows, width = out.shape
    group = rows + 2 * SIDE
    chunk = COL_DRIFT
    chunks = width // chunk
    p = lax.axis_index("patch")
    to_i = pltpu.make_async_copy(par_i, sm_i, sem)
    to_i.start()
    out[...] = jnp.zeros_like(out)
    count[...] = jnp.zeros_like(count)
    to_i.wait()
    passes, which = plan(p, np_, chunks)

    @pl.loop(0, passes)
    def _(q):
        c, dp = which(q)
        for dv, first, n, off in (
            (0, 0, rows, 0), (-1, 0, SIDE, rows), (1, rows - SIDE, SIDE, rows + SIDE)
        ):
            slot = slot_of(dv, dp)
            rs, cs, valid = sm_i[slot, 0, 0], sm_i[slot, 0, 1], sm_i[slot, 0, 2]
            y = lax.broadcasted_iota(I32, (n, LANES), 0) + (first - dv * rows) - rs
            live = jnp.logical_and(y >= 0, y < valid)
            turn = jnp.bitwise_and(cs, LANES - 1)
            l = lax.broadcasted_iota(I32, (n, LANES), 1)
            near = l < jnp.where(turn == 0, LANES, turn)
            block = (COL_DRIFT - cs) // LANES
            base = pl.multiple_of(block * LANES + c * chunk, LANES)
            x0 = l + (c * chunk - dp * width - cs)

            def turned(k):
                return pltpu.roll(moved[off : off + n, pl.ds(base + k * LANES, LANES)], turn, 1)

            former = turned(0)
            for k in range(chunk // LANES):
                later = turned(k + 1)
                value = jnp.where(near, former, later)
                former = later
                t, h = divmod(k, TILE // LANES)
                x = x0 + k * LANES
                mask = jnp.logical_and(live, jnp.logical_and(x >= 0, x < width))
                cv = conv[q, t * group + off : t * group + off + n, h * LANES : (h + 1) * LANES]
                here = pl.ds(pl.multiple_of(c * chunk + k * LANES, LANES), LANES)
                out[first : first + n, here] += jnp.where(mask, value - cv, 0.0)
                count[first : first + n, here] += jnp.where(mask, 1.0, 0.0)

    out[...] = out[...] / jnp.maximum(count[...], 1.0)


def body(np_, nv, template, science, row_shift, col_shift, valid_rows, basis_rows, basis_cols, terms):
    rows, width = template.shape
    terms_n = basis_rows.shape[0]
    group = rows + 2 * SIDE
    tiles = COL_DRIFT // TILE
    chunks = width // COL_DRIFT
    any_ = pl.BlockSpec(memory_space=pl.ANY)
    smem = pl.BlockSpec(memory_space=pltpu.SMEM)
    vmem = pl.BlockSpec(memory_space=pltpu.VMEM)
    conv, moved, par_i = pl.pallas_call(
        functools.partial(kernel, np_, nv),
        out_shape=(
            jax.ShapeDtypeStruct((chunks + 2, tiles * group, TILE), F32),
            jax.ShapeDtypeStruct((group, width + 2 * COL_DRIFT + LANES), F32),
            jax.ShapeDtypeStruct((9, 1, LANES), I32),
        ),
        in_specs=[any_, any_, smem, smem, smem, vmem, vmem, smem],
        out_specs=(vmem, vmem, vmem),
        scratch_shapes=[
            pltpu.VMEM((rows + 2 * TEDGE, width + 2 * LANES), BF16),
            pltpu.VMEM((rows + 2 * SEDGE, width + 2 * COL_DRIFT), BF16),
            pltpu.VMEM((9, 1, LANES), F32),
            pltpu.SMEM((9, 1, LANES), I32),
            pltpu.SMEM((9, 1, LANES), F32),
            pltpu.VMEM((2, 16, LANES), F32),
            pltpu.VMEM((terms_n * rows, LANES), BF16),
            pltpu.VMEM((2, terms_n * TILE, TILE), BF16),
            pltpu.VMEM(((tiles + 1) * group, terms_n * TILE), BF16),
            pltpu.SemaphoreType.DMA((4, 9)),
            pltpu.SemaphoreType.DMA((4, 9)),
            pltpu.SemaphoreType.DMA((4,)),
        ],
        compiler_params=pltpu.CompilerParams(
            collective_id=0, has_side_effects=True, vmem_limit_bytes=40 * 1024 * 1024
        ),
    )(template, science, row_shift, col_shift, valid_rows, basis_rows, basis_cols, terms)
    return pl.pallas_call(
        functools.partial(gather_kernel, np_),
        out_shape=jax.ShapeDtypeStruct((rows, width), F32),
        in_specs=[vmem, vmem, vmem],
        out_specs=vmem,
        scratch_shapes=[
            pltpu.VMEM((rows, width), F32),
            pltpu.SMEM((9, 1, LANES), I32),
            pltpu.SemaphoreType.DMA,
        ],
        compiler_params=pltpu.CompilerParams(vmem_limit_bytes=40 * 1024 * 1024),
    )(conv, moved, par_i)


def solution(mesh):
    placed = (
        P("visit", "patch"), P("visit", "patch"), P("visit", "patch"), P("visit", "patch"),
        P("visit", "patch"), P(), P(), P("visit", "patch", None),
    )
    run = functools.partial(body, mesh.shape["patch"], mesh.shape["visit"])
    return jax.shard_map(
        run, mesh=mesh, in_specs=placed, out_specs=P("visit", "patch"), check_vma=False
    )
```

time: 160 us -> 35.3 us (0.22)
  the two profiles are of different devices: /device:TPU:22 before, /device:TPU:17 now
where the time goes in v1:
time: 35.3 us; the launch traced here: 35 us
  Pallas kernels  29 us (82%)
  local copies, waits for them, and re-layouts  4.1 us (12%)
  between operations  1.96 us (6%)
    pallas_call x1, Pallas kernels, body(): pl.pallas_call(functools.partial(kernel, np_, nv), out_shape=(jax.ShapeDt...  25.8 us
    unnamed x10, local copies, waits for them, and re-layouts  4.1 us
    pallas_call x1, Pallas kernels, body(): pl.pallas_call(functools.partial(gather_kernel, np_), out_shape=jax.Shape...  3.16 us

profile of v1, /device:TPU:17, one launch (start us, length us, event | category | flops | bytes accessed | tf_op | source)
XLA Modules:
  0.0 35.0 jit_solution(5866283910951744168)
XLA Ops:
  1.9 0.0 copy-start
  2.0 1.0 %copy-done = bf16[64,4096]{1,0:T(8,128)(2,1)S(1)} copy-done((bf16[64,4096]{1,0:T(8,128)(2,1)S(1)}, bf16[64,4096]{1,0:T(8,128)(2,1)}, u32[]{:S(2)}) %copy-start) | copy-done | bytes 524312
  3.0 0.0 copy-start.1
  3.0 1.0 %copy-done.1 = bf16[64,4096]{1,0:T(8,128)(2,1)S(1)} copy-done((bf16[64,4096]{1,0:T(8,128)(2,1)S(1)}, bf16[64,4096]{1,0:T(8,128)(2,1)}, u32[]{:S(2)}) %copy-start.1) | copy-done | bytes 524312
  4.0 0.0 copy-start.2
  4.0 0.7 %copy-done.2 = bf16[9,21]{1,0:T(8,128)(2,1)S(1)} copy-done((bf16[9,21]{1,0:T(8,128)(2,1)S(1)}, bf16[9,21]{1,0:T(8,128)(2,1)}, u32[]{:S(2)}) %copy-start.2) | copy-done | bytes 402
  4.7 0.0 copy-start.3
  4.7 0.7 %copy-done.3 = bf16[9,21]{1,0:T(8,128)(2,1)S(1)} copy-done((bf16[9,21]{1,0:T(8,128)(2,1)S(1)}, bf16[9,21]{1,0:T(8,128)(2,1)}, u32[]{:S(2)}) %copy-start.3) | copy-done | bytes 402
  5.4 0.0 copy-start.4
  5.4 0.7 %copy-done.4 = f32[1,1,9]{2,1,0:T(1,128)S(1)} copy-done((f32[1,1,9]{2,1,0:T(1,128)S(1)}, f32[1,1,9]{2,1,0:T(1,128)}, u32[]{:S(2)}) %copy-start.4) | copy-done | bytes 60
  6.1 25.8 %shard_map.82 = (f32[6,448,256]{2,1,0:T(8,128)S(1)}, f32[112,6272]{1,0:T(8,128)S(1)}, s32[9,1,128]{2,1,0:T(1,128)S(1)}) custom-call(bf16[64,4096]{1,0:T(8,128)(2,1)S(1)} %copy-done, bf16[64,4096]{1,0:T(8,128)(2,1)S(1)} %copy-done.1, s32[1,1]{1,0:T(1,128)S(6)} %copy.9.row_shift, s32[1,1]{1,0:T(1,128)S(6)} %copy.10.col_shift, s32[1,1]{1,0:T(1,128)S(6)} %copy.11.valid_rows, ...), custom_call_target="tpu_custom_call" | custom-call | tf_op jit(solution)/shard_map/pallas_call | solution.py:300
  31.9 3.2 %shard_map.83 = f32[64,4096]{1,0:T(8,128)} custom-call(f32[6,448,256]{2,1,0:T(8,128)S(1)} %get-tuple-element.8.conv, f32[112,6272]{1,0:T(8,128)S(1)} %get-tuple-element.9.moved, s32[9,1,128]{2,1,0:T(1,128)S(1)} %get-tuple-element.10.par_i), custom_call_target="tpu_custom_call" | custom-call | tf_op jit(solution)/shard_map/pallas_call | solution.py:327
Async XLA Ops:
  1.9 1.0 %copy-start = (bf16[64,4096]{1,0:T(8,128)(2,1)S(1)}, bf16[64,4096]{1,0:T(8,128)(2,1)}, u32[]{:S(2)}) copy-start(bf16[64,4096]{1,0:T(8,128)(2,1)} %template.1) | copy-start | bytes 1572868
  3.0 1.0 %copy-start.1 = (bf16[64,4096]{1,0:T(8,128)(2,1)S(1)}, bf16[64,4096]{1,0:T(8,128)(2,1)}, u32[]{:S(2)}) copy-start(bf16[64,4096]{1,0:T(8,128)(2,1)} %science.1) | copy-start | bytes 1572868
  4.0 0.7 %copy-start.2 = (bf16[9,21]{1,0:T(8,128)(2,1)S(1)}, bf16[9,21]{1,0:T(8,128)(2,1)}, u32[]{:S(2)}) copy-start(bf16[9,21]{1,0:T(8,128)(2,1)} %basis_rows.1) | copy-start | bytes 1138
  4.7 0.7 %copy-start.3 = (bf16[9,21]{1,0:T(8,128)(2,1)S(1)}, bf16[9,21]{1,0:T(8,128)(2,1)}, u32[]{:S(2)}) copy-start(bf16[9,21]{1,0:T(8,128)(2,1)} %basis_cols.1) | copy-start | bytes 1138
  5.4 0.7 %copy-start.4 = (f32[1,1,9]{2,1,0:T(1,128)S(1)}, f32[1,1,9]{2,1,0:T(1,128)}, u32[]{:S(2)}) copy-start(f32[1,1,9]{2,1,0:T(1,128)} %terms.1) | copy-start | bytes 112

commit v2 on v1

--- a/solution.py
+++ b/solution.py
@@ -41,9 +41,9 @@
 
 
 def kernel(
-    np_, nv, template, science, row_shift, col_shift, valid_rows, basis_rows, basis_cols, terms,
-    conv, moved, par_i, text, sky, par_f, sm_i, sm_f, taps, band_v, band_h, weighted,
-    send_sem, recv_sem, local_sem,
+    np_, nv, template, science, row_shift, col_shift, valid_rows, basis_rows_hbm, basis_cols_hbm,
+    terms_hbm, conv, moved, par_i, basis_rows, basis_cols, terms, text, sky, par_f, sm_i, sm_f, taps, band_v, band_h, weighted,
+    conv_v, moved_v, par_v, send_sem, recv_sem, local_sem, out_sem,
 ):
     rows, width = template.shape
     terms_n, ksize = basis_rows.shape
@@ -63,18 +63,21 @@
                 ok = cond if ok is None else jnp.logical_and(ok, cond)
         return ok
 
+    small = [
+        pltpu.make_async_copy(a, b, local_sem.at[4 + i])
+        for i, (a, b) in enumerate(
+            ((terms_hbm, terms), (basis_rows_hbm, basis_rows), (basis_cols_hbm, basis_cols))
+        )
+    ]
+    for copy in small:
+        copy.start()
     lane = lax.broadcasted_iota(I32, (1, LANES), 1)
-    par_i[...] = jnp.zeros_like(par_i)
+    par_v[...] = jnp.zeros_like(par_v)
     par_f[...] = jnp.zeros_like(par_f)
     ints = jnp.where(
         lane == 0, row_shift[0, 0], jnp.where(lane == 1, col_shift[0, 0], jnp.where(lane == 2, valid_rows[0, 0], 0))
     )
-    par_i[4] = ints
-    floats = jnp.zeros((1, LANES), F32)
-    for b in range(terms_n):
-        floats = jnp.where(lane == b, terms[0, 0, b], floats)
-    par_f[4] = floats
-
+    par_v[4] = ints
     own_t = pltpu.make_async_copy(
         template, text.at[pl.ds(TEDGE, rows), pl.ds(LANES, width)], local_sem.at[0]
     )
@@ -83,6 +86,8 @@
     )
     own_t.start()
     own_s.start()
+    small[0].wait()
+    par_f[4, :, 0:terms_n] = terms[0]
 
     barrier = pltpu.get_barrier_semaphore()
     for dv, dp in AROUND:
@@ -101,7 +106,7 @@
 
     def regions(kind, dv, dp):
         if kind == 0:
-            return par_i.at[4], par_i.at[slot_of(dv, dp)]
+            return par_v.at[4], par_v.at[slot_of(dv, dp)]
         if kind == 1:
             return par_f.at[4], par_f.at[slot_of(dv, dp)]
         src, dst, re, ce = (
@@ -132,12 +137,14 @@
             device_id={"patch": p + dp, "visit": v + dv}, device_id_type=MESH,
         )
 
-    for kinds in ((0, 1, 2), (3,)):
-        for kind in kinds:
-            for ev, ep in AROUND:
-                @pl.when(there(ev, ep))
-                def _():
-                    sending(kind, ev, ep).start()
+    def send_all(kind):
+        for ev, ep in AROUND:
+            @pl.when(there(ev, ep))
+            def _():
+                sending(kind, ev, ep).start()
+
+    for kind in (0, 1, 2):
+        send_all(kind)
 
     for kind in (2, 3):
         for dv, dp in AROUND:
@@ -146,6 +153,8 @@
                 _, dst = regions(kind, dv, dp)
                 dst[...] = jnp.zeros(dst.shape, BF16)
 
+    small[1].wait()
+    small[2].wait()
     taps[...] = jnp.zeros_like(taps)
     taps[0, 0:terms_n, 0:ksize] = basis_rows[...].astype(F32)
     taps[1, 0:terms_n, 0:ksize] = basis_cols[...].astype(F32)
@@ -174,7 +183,8 @@
             @pl.when(there(dv, dp))
             def _():
                 receiving(kind, dv, dp).wait_recv()
-    to_i = pltpu.make_async_copy(par_i, sm_i, local_sem.at[2])
+    send_all(3)
+    to_i = pltpu.make_async_copy(par_v, sm_i, local_sem.at[2])
     to_f = pltpu.make_async_copy(par_f, sm_f, local_sem.at[3])
     to_i.start()
     to_f.start()
@@ -203,11 +213,12 @@
                 weighted[at + rows : at + group, b * TILE : (b + 1) * TILE] = jnp.concatenate(
                     [blk[:SIDE] * up_w, blk[rows - SIDE :] * down_w], axis=0
                 ).astype(BF16)
-        conv[q] = jnp.dot(
+        conv_v[q] = jnp.dot(
             weighted[0 : tiles * group, :], band_h[0], preferred_element_type=F32
         ) + jnp.dot(
             weighted[group : (tiles + 1) * group, :], band_h[1], preferred_element_type=F32
         )
+        pltpu.make_async_copy(conv_v.at[q], conv.at[q], out_sem.at[q]).start()
 
     own_s.wait()
     for dv, dp in AROUND:
@@ -217,44 +228,79 @@
 
     def pick(dp):
         parts = []
-        for dv, first, n in ((0, 0, rows), (-1, 0, SIDE), (1, rows - SIDE, SIDE)):
+        for dv, first, n in ((0, 0, rows), (-1, 0, SEDGE), (1, rows - SEDGE, SEDGE)):
             y = lax.broadcasted_iota(I32, (n, rows + 2 * SEDGE), 0) + first
             j = lax.broadcasted_iota(I32, (n, rows + 2 * SEDGE), 1)
             rs = sm_i[slot_of(dv, dp), 0, 0]
             parts.append((j == y + SEDGE - rs).astype(F32))
         return jnp.concatenate(parts, axis=0).astype(BF16)
 
-    for dp, first, n in ((-1, 0, COL_DRIFT), (0, COL_DRIFT, width), (1, COL_DRIFT + width, COL_DRIFT)):
+    par_out = pltpu.make_async_copy(par_v, par_i, local_sem.at[2])
+    par_out.start()
+    leaving = [par_out]
+    halfway = width // 2
+    for i, (dp, first, n) in enumerate((
+        (-1, 0, COL_DRIFT), (0, COL_DRIFT, halfway), (0, COL_DRIFT + halfway, halfway),
+        (1, COL_DRIFT + width, COL_DRIFT),
+    )):
         chosen = pick(dp)
-        for k in range(n // TILE):
-            at = first + k * TILE
-            moved[:, at : at + TILE] = jnp.dot(
+        for t in range(n // TILE):
+            at = first + t * TILE
+            moved_v[:, at : at + TILE] = jnp.dot(
                 chosen, sky[:, at : at + TILE], preferred_element_type=F32
-            )
+            ).astype(BF16)
+        part = (slice(None), pl.ds(first, n))
+        copy = pltpu.make_async_copy(moved_v.at[part], moved.at[part], out_sem.at[chunks + 2 + i])
+        copy.start()
+        leaving.append(copy)
 
     for kind in range(4):
         for ev, ep in AROUND:
             @pl.when(there(ev, ep))
             def _():
                 sending(kind, ev, ep).wait_send()
-
-
-def gather_kernel(np_, conv, moved, par_i, out, count, sm_i, sem):
-    rows, width = out.shape
+    for copy in leaving:
+        copy.wait()
+
+    @pl.loop(0, passes)
+    def _(q):
+        pltpu.make_async_copy(conv_v.at[q], conv.at[q], out_sem.at[q]).wait()
+
+
+def gather_kernel(
+    np_, conv_h, moved_h, par_i, out_h, conv, moved, out, count, sm_i, sem, conv_sem, moved_sem, out_sem
+):
+    rows, width = out_h.shape
     group = rows + 2 * SIDE
     chunk = COL_DRIFT
     chunks = width // chunk
     p = lax.axis_index("patch")
     to_i = pltpu.make_async_copy(par_i, sm_i, sem)
     to_i.start()
+    bring = []
+    halfway = width // 2
+    for i, (first, n) in enumerate((
+        (0, chunk), (chunk, halfway), (chunk + halfway, halfway), (chunk + width, chunk)
+    )):
+        part = (slice(None), pl.ds(first, n))
+        bring.append(pltpu.make_async_copy(moved_h.at[part], moved.at[part], moved_sem.at[i]))
+        bring[-1].start()
+    passes, which = plan(p, np_, chunks)
+
+    @pl.loop(0, passes)
+    def _(q):
+        pltpu.make_async_copy(conv_h.at[q], conv.at[q], conv_sem.at[q]).start()
+
     out[...] = jnp.zeros_like(out)
     count[...] = jnp.zeros_like(count)
     to_i.wait()
-    passes, which = plan(p, np_, chunks)
+    for copy in bring:
+        copy.wait()
 
     @pl.loop(0, passes)
     def _(q):
         c, dp = which(q)
+        pltpu.make_async_copy(conv_h.at[q], conv.at[q], conv_sem.at[q]).wait()
         for dv, first, n, off in (
             (0, 0, rows, 0), (-1, 0, SIDE, rows), (1, rows - SIDE, SIDE, rows + SIDE)
         ):
@@ -262,6 +308,8 @@
             rs, cs, valid = sm_i[slot, 0, 0], sm_i[slot, 0, 1], sm_i[slot, 0, 2]
             y = lax.broadcasted_iota(I32, (n, LANES), 0) + (first - dv * rows) - rs
             live = jnp.logical_and(y >= 0, y < valid)
+            src, src_n = {0: (0, rows), -1: (rows, SEDGE), 1: (rows + SEDGE, SEDGE)}[dv]
+            skip = SEDGE - SIDE if dv == 1 else 0
             turn = jnp.bitwise_and(cs, LANES - 1)
             l = lax.broadcasted_iota(I32, (n, LANES), 1)
             near = l < jnp.where(turn == 0, LANES, turn)
@@ -270,7 +318,8 @@
             x0 = l + (c * chunk - dp * width - cs)
 
             def turned(k):
-                return pltpu.roll(moved[off : off + n, pl.ds(base + k * LANES, LANES)], turn, 1)
+                got = moved[src : src + src_n, pl.ds(base + k * LANES, LANES)].astype(F32)
+                return pltpu.roll(got[skip : skip + n], turn, 1)
 
             former = turned(0)
             for k in range(chunk // LANES):
@@ -285,7 +334,14 @@
                 out[first : first + n, here] += jnp.where(mask, value - cv, 0.0)
                 count[first : first + n, here] += jnp.where(mask, 1.0, 0.0)
 
-    out[...] = out[...] / jnp.maximum(count[...], 1.0)
+    leaving = []
+    for c in range(chunks):
+        part = (slice(None), pl.ds(c * chunk, chunk))
+        out[part] = out[part] / jnp.maximum(count[part], 1.0)
+        leaving.append(pltpu.make_async_copy(out.at[part], out_h.at[part], out_sem.at[c]))
+        leaving[-1].start()
+    for copy in leaving:
+        copy.wait()
 
 
 def body(np_, nv, template, science, row_shift, col_shift, valid_rows, basis_rows, basis_cols, terms):
@@ -294,19 +350,21 @@
     group = rows + 2 * SIDE
     tiles = COL_DRIFT // TILE
     chunks = width // COL_DRIFT
-    any_ = pl.BlockSpec(memory_space=pl.ANY)
+    hbm = pl.BlockSpec(memory_space=pltpu.HBM)
     smem = pl.BlockSpec(memory_space=pltpu.SMEM)
-    vmem = pl.BlockSpec(memory_space=pltpu.VMEM)
     conv, moved, par_i = pl.pallas_call(
         functools.partial(kernel, np_, nv),
         out_shape=(
             jax.ShapeDtypeStruct((chunks + 2, tiles * group, TILE), F32),
-            jax.ShapeDtypeStruct((group, width + 2 * COL_DRIFT + LANES), F32),
+            jax.ShapeDtypeStruct((rows + 2 * SEDGE, width + 2 * COL_DRIFT + LANES), BF16),
             jax.ShapeDtypeStruct((9, 1, LANES), I32),
         ),
-        in_specs=[any_, any_, smem, smem, smem, vmem, vmem, smem],
-        out_specs=(vmem, vmem, vmem),
+        in_specs=[hbm, hbm, smem, smem, smem, hbm, hbm, hbm],
+        out_specs=(hbm, hbm, hbm),
         scratch_shapes=[
+            pltpu.VMEM(basis_rows.shape, BF16),
+            pltpu.VMEM(basis_cols.shape, BF16),
+            pltpu.VMEM(terms.shape, F32),
             pltpu.VMEM((rows + 2 * TEDGE, width + 2 * LANES), BF16),
             pltpu.VMEM((rows + 2 * SEDGE, width + 2 * COL_DRIFT), BF16),
             pltpu.VMEM((9, 1, LANES), F32),
@@ -316,25 +374,35 @@
             pltpu.VMEM((terms_n * rows, LANES), BF16),
             pltpu.VMEM((2, terms_n * TILE, TILE), BF16),
             pltpu.VMEM(((tiles + 1) * group, terms_n * TILE), BF16),
+            pltpu.VMEM((chunks + 2, tiles * group, TILE), F32),
+            pltpu.VMEM((rows + 2 * SEDGE, width + 2 * COL_DRIFT + LANES), BF16),
+            pltpu.VMEM((9, 1, LANES), I32),
             pltpu.SemaphoreType.DMA((4, 9)),
             pltpu.SemaphoreType.DMA((4, 9)),
-            pltpu.SemaphoreType.DMA((4,)),
+            pltpu.SemaphoreType.DMA((7,)),
+            pltpu.SemaphoreType.DMA((chunks + 6,)),
         ],
         compiler_params=pltpu.CompilerParams(
-            collective_id=0, has_side_effects=True, vmem_limit_bytes=40 * 1024 * 1024
+            collective_id=0, has_side_effects=True, vmem_limit_bytes=58 * 1024 * 1024
         ),
     )(template, science, row_shift, col_shift, valid_rows, basis_rows, basis_cols, terms)
     return pl.pallas_call(
         functools.partial(gather_kernel, np_),
         out_shape=jax.ShapeDtypeStruct((rows, width), F32),
-        in_specs=[vmem, vmem, vmem],
-        out_specs=vmem,
+        in_specs=[hbm, hbm, hbm],
+        out_specs=hbm,
         scratch_shapes=[
+            pltpu.VMEM((chunks + 2, tiles * group, TILE), F32),
+            pltpu.VMEM((rows + 2 * SEDGE, width + 2 * COL_DRIFT + LANES), BF16),
+            pltpu.VMEM((rows, width), F32),
             pltpu.VMEM((rows, width), F32),
             pltpu.SMEM((9, 1, LANES), I32),
             pltpu.SemaphoreType.DMA,
+            pltpu.SemaphoreType.DMA((chunks + 2,)),
+            pltpu.SemaphoreType.DMA((4,)),
+            pltpu.SemaphoreType.DMA((chunks,)),
         ],
-        compiler_params=pltpu.CompilerParams(vmem_limit_bytes=40 * 1024 * 1024),
+        compiler_params=pltpu.CompilerParams(vmem_limit_bytes=58 * 1024 * 1024),
     )(conv, moved, par_i)
 
 

time: 35.3 us -> 28.9 us (0.82)
  local copies, waits for them, and re-layouts: 4.1 us -> 0 us
  Pallas kernels: 29 us -> 26.8 us
    unnamed x10 -> x0, local copies, waits for them, and re-layouts: 4.1 us -> none
    pallas_call x1, Pallas kernels: 25.8 us -> 22.8 us  [body(): pl.pallas_call(functools.partial(kernel, np_, nv), out_shape=(jax.ShapeDt...]
    pallas_call x1, Pallas kernels: 3.16 us -> 3.97 us  [body(): pl.pallas_call(functools.partial(gather_kernel, np_), out_shape=jax.Shape...]
where the time goes in v2:
time: 28.9 us; the launch traced here: 28.8 us
  Pallas kernels  26.8 us (93%)
  between operations  1.95 us (7%)
    pallas_call x1, Pallas kernels, body(): pl.pallas_call(functools.partial(kernel, np_, nv), out_shape=(jax.ShapeDt...  22.8 us
    pallas_call x1, Pallas kernels, body(): pl.pallas_call(functools.partial(gather_kernel, np_), out_shape=jax.Shape...  3.97 us

profile of v2, /device:TPU:17, one launch (start us, length us, event | category | flops | bytes accessed | tf_op | source)
XLA Modules:
  0.0 28.8 jit_solution(15220470499739387645)
XLA Ops:
  1.9 22.8 %shard_map.82 = (f32[6,448,256]{2,1,0:T(8,128)}, bf16[128,6272]{1,0:T(8,128)(2,1)}, s32[9,1,128]{2,1,0:T(1,128)}) custom-call(bf16[64,4096]{1,0:T(8,128)(2,1)} %template.1, bf16[64,4096]{1,0:T(8,128)(2,1)} %science.1, s32[1,1]{1,0:T(1,128)S(6)} %copy.9.row_shift, s32[1,1]{1,0:T(1,128)S(6)} %copy.10.col_shift, s32[1,1]{1,0:T(1,128)S(6)} %copy.11.valid_rows, ...), custom_call_target="tpu_custom_call" | custom-call | tf_op jit(solution)/shard_map/pallas_call | solution.py:355
  24.8 4.0 %shard_map.83 = f32[64,4096]{1,0:T(8,128)} custom-call(f32[6,448,256]{2,1,0:T(8,128)} %get-tuple-element.8.conv_h, bf16[128,6272]{1,0:T(8,128)(2,1)} %get-tuple-element.9.moved_h, s32[9,1,128]{2,1,0:T(1,128)} %get-tuple-element.10.par_i), custom_call_target="tpu_custom_call" | custom-call | tf_op jit(solution)/shard_map/pallas_call | solution.py:389
